TPU v7x, 128 devices: a whole 4x4x4 slice. The times are simulated.
128 devices in a mesh: row: 8 (over z, core), col: 16 (over x, y).
Axes of the slice: x: 4, y: 4, z: 4, core: 2. Of those that a mesh axis runs over, the one named last changes fastest.
Arguments:
- tile_values: bfloat16 [8, 16, 40, 512, 512], P('row', 'col')
- tile_rows: int32 [8, 16, 40], P('row', 'col'), may hold values from 0 to 31
- tile_cols: int32 [8, 16, 40], P('row', 'col'), may hold values from 0 to 15
- start_basis: bfloat16 [131072, 256], P(('row', 'col')), may hold values from -6 to 6
Outputs:
- new_basis: float32 [131072, 256], P(('row', 'col'))
- triangle: float32 [256, 256], replicated
All inputs are finite; a program needn't handle non-finite values.
Results may differ from a plain program's by a relative error of at most 0.002.
Values may be sent and summed in bfloat16 or wider, within the bound.
No kernel may reach another device: no remote copies, remote signals or barrier semaphores. Data moves between devices by JAX's collectives and lax.ppermute only.
A program may use at most 192 MiB of HBM per device.

v0:
```python
import jax
import jax.numpy as jnp
from jax import lax
from jax.sharding import PartitionSpec as P

ORDER = 131072


def per_device(tile_values, tile_rows, tile_cols, start_basis):
    local_tiles = tile_values[0, 0]
    row_ids = tile_rows[0, 0]
    col_ids = tile_cols[0, 0]
    block_size = local_tiles.shape[1]
    rank_size = start_basis.shape[1]
    row_count = lax.axis_size("row")
    col_count = lax.axis_size("col")
    gathered = lax.all_gather(start_basis, "col", axis=0, tiled=True).reshape(
        -1, block_size, rank_size
    )
    row_blocks = gathered.shape[0]
    col_blocks = row_blocks * row_count // col_count
    picked = jnp.take(gathered, row_ids, axis=0)
    product = jnp.einsum("ktn,ktr->knr", local_tiles, picked, preferred_element_type=jnp.float32)
    col_onehot = (col_ids[:, None] == jnp.arange(col_blocks, dtype=jnp.int32)[None, :]).astype(
        jnp.float32
    )
    partial_value = jnp.einsum("kc,knr->cnr", col_onehot, product, precision=lax.Precision.HIGHEST)
    wide_blocks = lax.psum(partial_value, "row").astype(jnp.bfloat16)
    selected = jnp.take(wide_blocks, col_ids, axis=0)
    second_product = jnp.einsum(
        "kmn,knr->kmr", local_tiles, selected, preferred_element_type=jnp.float32
    )
    row_onehot = (row_ids[:, None] == jnp.arange(row_blocks, dtype=jnp.int32)[None, :]).astype(
        jnp.float32
    )
    row_partial = jnp.einsum(
        "kb,kmr->bmr", row_onehot, second_product, precision=lax.Precision.HIGHEST
    )
    image_rows = lax.psum_scatter(row_partial, "col", scatter_dimension=0, tiled=True).reshape(
        -1, rank_size
    )
    local_gram = jnp.dot(image_rows.T, image_rows, precision=lax.Precision.HIGHEST)
    gram_matrix = lax.psum(local_gram, ("row", "col")) / ORDER
    lower_factor = jnp.linalg.cholesky(gram_matrix)
    new_basis = jax.scipy.linalg.solve_triangular(lower_factor, image_rows.T, lower=True).T
    return (new_basis, lower_factor.T)


def solution(mesh):
    in_specs = (
        P("row", "col", None, None, None),
        P("row", "col", None),
        P("row", "col", None),
        P(("row", "col"), None),
    )
    out_specs = (P(("row", "col"), None), P())
    return jax.shard_map(
        per_device, mesh=mesh, in_specs=in_specs, out_specs=out_specs, check_vma=False
    )
```

profile of v0, /device:TPU:0, one launch (start us, length us, event | category | flops | bytes accessed | tf_op | source)
XLA Modules:
  0.0 656.4 jit_solution(11640249403922157854)
XLA Ops:
  10.6 72.6 %all-gather.2.cloned.1.call-done = bf16[16384,256]{1,0:T(8,128)(2,1)} async-done(((bf16[1024,256]{1,0:T(8,128)(2,1)}), bf16[16384,256]{1,0:T(8,128)(2,1)}) %all-gather.2.cloned.1.call-update) | async-done | bytes 8388624 | tf_op jit(solution)/shard_map/all_gather | solution.py:17
  83.2 9.1 %gather_fusion = bf16[40,512,256]{2,1,0:T(8,128)(2,1)} fusion(bf16[32,512,256]{2,1,0:T(8,128)(2,1)} %bitcast.75, s32[1024]{0:T(1024)S(1)} %pad_clamp_fusion.1), kind=kCustom, calls=%fused_computation | custom fusion | bytes 20971680 | tf_op jit(solution)/shard_map/jit(_take)/gather | solution.py:22
  92.4 19.4 %fusion.8 = f32[40,512,256]{1,2,0:T(8,128)} fusion(bf16[1,1,40,512,512]{4,3,2,1,0:T(8,128)(2,1)} %param.4, bf16[40,512,256]{2,1,0:T(8,128)(2,1)} %gather_fusion, pred[40]{0:T(512)(128)(4,1)S(1)} %compare_and_fusion), kind=kOutput, calls=%fused_computation.12 | convolution fusion | flops 5373952000 | bytes 52428840 | tf_op jit(solution)/shard_map/ktn,ktr->knr/dot_general | solution.py:23
  111.8 22.3 %copy.31 = f32[40,512,256]{2,0,1:T(8,128)} copy(f32[40,512,256]{1,2,0:T(8,128)} %fusion.8) | data formatting | bytes 41943040 | tf_op jit(solution)/shard_map/ktn,ktr->knr/dot_general | solution.py:23
  134.1 13.5 %fusion.35 = f32[16,512,256]{2,0,1:T(8,128)} fusion(f32[40,512,256]{2,0,1:T(8,128)} %copy.31, s32[40]{0:T(128)S(1)} %bitcast.80), kind=kOutput, calls=%fused_computation.47 | convolution fusion | flops 1006633600 | bytes 29360288 | tf_op jit(solution)/shard_map/kc,knr->cnr/dot_general | solution.py:27
  147.6 93.0 %all-reduce.5 = bf16[16,512,256]{2,0,1:T(8,128)(2,1)} all-reduce(f32[16,512,256]{2,0,1:T(8,128)} %fusion.35), channel_id=1, replica_groups=mesh['row'=8,'col'=16] {'row'}, use_global_device_ids=true, to_apply=%region_0.1 | all-reduce | flops 2097152 | bytes 12582912 | tf_op jit(solution)/shard_map/psum | solution.py:28
  240.6 5.6 copy.32
  246.2 7.9 %gather_fusion.1 = bf16[40,512,256]{2,1,0:T(8,128)(2,1)} fusion(bf16[16,512,256]{2,1,0:T(8,128)(2,1)} %copy.32, s32[1024]{0:T(1024)S(1)} %pad_clamp_fusion), kind=kCustom, calls=%fused_computation.1 | custom fusion | bytes 20971680 | tf_op jit(solution)/shard_map/jit(_take)/gather | solution.py:29
  254.1 19.6 %fusion.13 = f32[40,512,256]{1,2,0:T(8,128)} fusion(bf16[1,1,40,512,512]{4,3,2,1,0:T(8,128)(2,1)} %param.4, bf16[40,512,256]{2,1,0:T(8,128)(2,1)} %gather_fusion.1, pred[40]{0:T(512)(128)(4,1)S(1)} %compare_and_fusion.1), kind=kOutput, calls=%fused_computation.13 | convolution fusion | flops 5373952000 | bytes 52428840 | tf_op jit(solution)/shard_map/kmn,knr->kmr/dot_general | solution.py:30
  273.7 22.3 %copy.34 = f32[40,512,256]{2,0,1:T(8,128)} copy(f32[40,512,256]{1,2,0:T(8,128)} %fusion.13) | data formatting | bytes 41943040 | tf_op jit(solution)/shard_map/kmn,knr->kmr/dot_general | solution.py:30
  296.0 16.7 %fusion.31 = f32[32,512,256]{2,0,1:T(8,128)} fusion(f32[40,512,256]{2,0,1:T(8,128)} %copy.34, s32[40]{0:T(128)S(1)} %bitcast.79), kind=kOutput, calls=%fused_computation.43 | convolution fusion | flops 2013267200 | bytes 37748896 | tf_op jit(solution)/shard_map/kb,kmr->bmr/dot_general | solution.py:36
  312.7 15.8 %copy.35 = f32[32,512,256]{2,1,0:T(8,128)} copy(f32[32,512,256]{2,0,1:T(8,128)} %fusion.31) | data formatting | bytes 33554432 | tf_op jit(solution)/shard_map/kb,kmr->bmr/dot_general | solution.py:36
  328.8 107.7 %reduce-scatter.2.cloned.1.call-done = f32[2,512,256]{2,1,0:T(8,128)} async-done(((f32[32,512,256]{2,1,0:T(8,128)}), f32[2,512,256]{2,1,0:T(8,128)}) %reduce-scatter.2.cloned.1.call-update) | async-done | bytes 1048592 | tf_op jit(solution)/shard_map/reduce_scatter | solution.py:39
  436.5 4.1 convolution_bitcast_fusion
  440.6 1.6 copy.39
  442.2 141.2 %all-reduce.4.cloned.1.call-done = f32[256,256]{0,1:T(8,128)} async-done(((f32[256,256]{0,1:T(8,128)}), f32[256,256]{0,1:T(8,128)}) %all-reduce.4.cloned.1.call-update) | async-done | bytes 262160 | tf_op jit(solution)/shard_map/psum | solution.py:43
  585.5 11.7 %cholesky.50 = f32[128,128]{1,0:T(8,128)S(1)} custom-call(f32[128,128]{1,0:T(8,128)S(1)} %cholesky.118), custom_call_target="Cholesky" | custom-call | tf_op jit(solution)/shard_map/jit(cholesky)/cholesky | solution.py:44
  597.3 9.8 %custom-call.15 = f32[1,128,128]{1,2,0:T(8,128)S(1)} custom-call(f32[1,128,128]{2,1,0:T(8,128)S(1)} %get-tuple-element.33), custom_call_target="InvertDiagBlocksLowerTriangular" | custom-call | tf_op jit(solution)/shard_map/jit(cholesky)/cholesky | solution.py:44
  607.6 11.9 %cholesky.105 = f32[128,128]{1,0:T(8,128)S(1)} custom-call(f32[128,128]{1,0:T(8,128)S(1)} %convolution_subtract_fusion.1), custom_call_target="Cholesky" | custom-call | tf_op jit(solution)/shard_map/jit(cholesky)/cholesky | solution.py:44
  621.7 4.1 while.1
  622.3 1.4 bitcast_dynamic-update-slice_fusion.2
  624.4 1.4 bitcast_dynamic-update-slice_fusion.2
  625.8 19.7 %custom-call.16 = f32[2,128,128]{1,2,0:T(8,128)S(1)} custom-call(f32[2,128,128]{2,1,0:T(8,128)S(1)} %get-tuple-element.9), custom_call_target="InvertDiagBlocksLowerTriangular" | custom-call | tf_op jit(solution)/shard_map/jit(_solve_triangular)/triangular_solve | solution.py:45
  647.5 1.3 copy.40
  (39 shorter events, 11.1 us)
Async XLA Ops:
  7.2 76.1 %all-gather.2.cloned.1.call-start = ((), (), s32[]{:S(2)}) async-start(), calls=%async_computation.1 | async-start | bytes 8912896 | tf_op jit(solution)/shard_map/all_gather | solution.py:17
  7.9 428.6 %reduce-scatter.2.cloned.1.call-start = ((), (), s32[]{:S(2)}) async-start(), calls=%async_computation.2 | async-start | bytes 17825792 | tf_op jit(solution)/shard_map/reduce_scatter | solution.py:39
  111.8 22.3 %copy-start.1 = (s32[1,1,40]{2,1,0:T(1,128)S(1)}, s32[1,1,40]{2,1,0:T(1,128)}, u32[]{:S(2)}) copy-start(s32[1,1,40]{2,1,0:T(1,128)} %param.6) | copy-start | bytes 484
  273.7 22.3 %copy-start = (s32[1,1,40]{2,1,0:T(1,128)S(1)}, s32[1,1,40]{2,1,0:T(1,128)}, u32[]{:S(2)}) copy-start(s32[1,1,40]{2,1,0:T(1,128)} %param.5) | copy-start | bytes 484
  328.6 254.9 %all-reduce.4.cloned.1.call-start = ((), (), s32[]{:S(2)}) async-start(), calls=%async_computation.3 | async-start | bytes 524288 | tf_op jit(solution)/shard_map/psum | solution.py:43
Sparse Core Ops, SparseCore 0:
  10.1 73.0 all-gather.1
  328.7 107.7 reduce-scatter.1
  441.8 141.5 all-reduce.3
where the time goes:
time: 664 us; the launch traced here: 656 us
  waiting for transfers between devices  322 us (48%)
  blocking collectives  93 us (14%)
  local copies, waits for them, and re-layouts  91.1 us (14%)
  matrix products  75.5 us (11%)
  other arithmetic  58.6 us (9%)
  between operations  15.4 us (2%)
    psum x1, waiting for transfers between devices, per_device(): gram_matrix = lax.psum(local_gram, ('row', 'col')) / ORDER  141 us
    reduce_scatter x1, waiting for transfers between devices, per_device(): lax.psum_scatter(row_partial, 'col', scatter_dimension=0, tiled=True)  108 us
    psum x1, blocking collectives, per_device(): wide_blocks = lax.psum(partial_value, 'row').astype(jnp.bfloat16)  93 us
    all_gather x1, waiting for transfers between devices, per_device(): lax.all_gather(start_basis, 'col', axis=0, tiled=True)  72.6 us
    another operation x6, other arithmetic, per_device(): lower_factor = jnp.linalg.cholesky(gram_matrix)  34.2 us
    dot_general x1, local copies, waits for them, and re-layouts, per_device(): jnp.einsum('ktn,ktr->knr', local_tiles, picked, preferred_element_type=jn...  22.3 us
    dot_general x1, local copies, waits for them, and re-layouts, per_device(): jnp.einsum('kmn,knr->kmr', local_tiles, selected, preferred_element_type=...  22.3 us
    another operation x2, other arithmetic, per_device(): jax.scipy.linalg.solve_triangular(lower_factor, image_rows.T, lower=True)  19.7 us
  transfers between devices with their start and end apart: 3, of which 3 were waited for; matrix products, arithmetic and copies ran while one was open for 1% of the time, Pallas kernels for 0%

commit v1 on v0

v1 whole, which is shorter than its diff:
```python
import functools

import jax
import jax.numpy as jnp
from jax import lax
from jax.experimental import pallas as pl
from jax.experimental.pallas import tpu as pltpu
from jax.sharding import PartitionSpec as P

ORDER = 131072
TB = 512
CHUNKS = 1
STEP = 4
PAD = 16
TINY = 1e-30
LIMIT = 60 * 2**20
VMEM = pl.BlockSpec(memory_space=pltpu.VMEM)
ANY = pl.BlockSpec(memory_space=pl.ANY)
F32 = jnp.float32

HOPS = (1, 3, 2)


def permute(value, axis, hop):
    if axis in ("z", "core"):
        name, size = "row", 8
        place = (lambda i: (i + 2 * hop) % 8) if axis == "z" else (lambda i: i ^ 1)
    else:
        name, size = "col", 16
        if axis == "x":
            place = lambda i: (i + 4 * hop) % 16
        else:
            place = lambda i: i // 4 * 4 + (i + hop) % 4
    return lax.ppermute(value, name, [(i, place(i)) for i in range(size)])


def slot_to(distance):
    return jnp.where(distance >= 2, 5 - distance, distance)


def slot_from(distance):
    return slot_to((4 - distance) % 4)


def params(**kw):
    return pltpu.CompilerParams(vmem_limit_bytes=LIMIT, **kw)


def exponent(top):
    return jnp.ceil(jnp.log2(jnp.maximum(top, TINY)) + 0.01) - 15.0


def code(value):
    power = exponent(jnp.max(jnp.abs(value), axis=0, keepdims=True))
    return jnp.round(value * jnp.exp2(-power)).astype(jnp.int16), power


def store_coded(ref, blocks):
    powers = []
    for i, value in enumerate(blocks):
        m = value.shape[0]
        ref[i * m : (i + 1) * m, :], power = code(value)
        powers.append(power)
    fill = jnp.zeros((PAD - len(powers), powers[0].shape[1]), F32)
    ref[-PAD:, :] = jnp.concatenate(powers + [fill], axis=0).astype(jnp.int16)


def units(ref):
    return jnp.exp2(ref[-PAD:, :].astype(F32))


def first_product(rows, cols, tiles, pieces, m):
    count = tiles.shape[0]
    n = len(pieces)

    def body(row_ref, col_ref, tile_ref, *rest):
        ins, keep_ref, send_ref, basis, acc, sems = (
            rest[:n],
            rest[n],
            rest[n + 1],
            rest[n + 2],
            rest[n + 3],
            rest[n + 4],
        )
        step = pl.program_id(0)

        @pl.when(step == 0)
        def _():
            copies = [
                pltpu.make_async_copy(ins[i], basis.at[pl.ds(4 * i, 4)], sems.at[i])
                for i in range(n)
            ]
            for copy in copies:
                copy.start()
            acc[...] = jnp.zeros_like(acc)
            for copy in copies:
                copy.wait()

        for j in range(STEP):
            k = step * STEP + j
            acc[col_ref[k]] += jnp.dot(
                basis[row_ref[k]], tile_ref[j], preferred_element_type=F32
            )

        @pl.when(step == count // STEP - 1)
        def _():
            first = pltpu.make_async_copy(acc.at[pl.ds(0, 8)], keep_ref, sems.at[0])
            second = pltpu.make_async_copy(acc.at[pl.ds(8, 8)], send_ref, sems.at[1])
            second.start()
            first.start()
            second.wait()
            first.wait()

    half = jax.ShapeDtypeStruct((8, m, TB), F32)
    return pl.pallas_call(
        body,
        grid_spec=pltpu.PrefetchScalarGridSpec(
            num_scalar_prefetch=2,
            grid=(count // STEP,),
            in_specs=[pl.BlockSpec((STEP, TB, TB), lambda i, *_: (i, 0, 0))] + [ANY] * n,
            out_specs=[ANY, ANY],
            scratch_shapes=[
                pltpu.VMEM((4 * n, m, TB), jnp.bfloat16),
                pltpu.VMEM((16, m, TB), F32),
                pltpu.SemaphoreType.DMA((n,)),
            ],
        ),
        out_shape=[half, half],
        compiler_params=params(),
        cost_estimate=pl.CostEstimate(
            flops=2 * count * TB * TB * m, bytes_accessed=36 * 2**20, transcendentals=0
        ),
        name="first_product",
    )(rows, cols, tiles, *pieces)


def second_product(rows, cols, tiles, pieces, m):
    count = tiles.shape[0]
    n = len(pieces)

    def body(row_ref, col_ref, tile_ref, *rest):
        ins, outs = rest[:n], rest[n : n + 8]
        wide, acc, sems = rest[n + 8 :]
        step = pl.program_id(0)

        @pl.when(step == 0)
        def _():
            copies = [
                pltpu.make_async_copy(ins[i], wide.at[pl.ds(2 * i, 2)], sems.at[i])
                for i in range(n)
            ]
            for copy in copies:
                copy.start()
            acc[...] = jnp.zeros_like(acc)
            for copy in copies:
                copy.wait()

        for j in range(STEP):
            k = step * STEP + j
            acc[row_ref[k]] += lax.dot_general(
                wide[col_ref[k]],
                tile_ref[j],
                (((1,), (1,)), ((), ())),
                preferred_element_type=F32,
            )

        @pl.when(step == count // STEP - 1)
        def _():
            for i in range(8):
                store_coded(outs[i], [acc[4 * i + b] for b in range(4)])

    out = jax.ShapeDtypeStruct((4 * m + PAD, TB), jnp.int16)
    return pl.pallas_call(
        body,
        grid_spec=pltpu.PrefetchScalarGridSpec(
            num_scalar_prefetch=2,
            grid=(count // STEP,),
            in_specs=[pl.BlockSpec((STEP, TB, TB), lambda i, *_: (i, 0, 0))] + [ANY] * n,
            out_specs=[VMEM] * 8,
            scratch_shapes=[
                pltpu.VMEM((2 * n, m, TB), jnp.bfloat16),
                pltpu.VMEM((32, m, TB), F32),
                pltpu.SemaphoreType.DMA((n,)),
            ],
        ),
        out_shape=[out] * 8,
        compiler_params=params(),
        cost_estimate=pl.CostEstimate(
            flops=2 * count * TB * TB * m, bytes_accessed=36 * 2**20, transcendentals=0
        ),
        name="second_product",
    )(rows, cols, tiles, *pieces)


def pair_sum(keep, other, m):
    def body(keep_ref, other_ref, *rest):
        i = pl.program_id(0)
        outs, buf = rest[:4], rest[4]
        for s in range(4):

            @pl.when(i == s)
            def _(s=s):
                store_coded(outs[s], [keep_ref[b] + other_ref[b] for b in range(2)])

    out = jax.ShapeDtypeStruct((2 * m + PAD, TB), jnp.int16)
    block = pl.BlockSpec((2, m, TB), lambda i: (i, 0, 0))
    return pl.pallas_call(
        body,
        grid=(4,),
        in_specs=[block, block],
        out_specs=[VMEM] * 4,
        out_shape=[out] * 4,
        scratch_shapes=[pltpu.VMEM((8, 128), F32)],
        compiler_params=params(),
        name="pair_sum",
    )(keep, other)


def decoded_sum(refs, b, m):
    total = None
    for ref in refs:
        part = ref[b * m : (b + 1) * m, :].astype(F32) * units(ref)[b : b + 1, :]
        total = part if total is None else total + part
    return total


def wide_sum(parts, m):
    def body(*refs):
        for b in range(2):
            refs[4][b] = decoded_sum(refs[:4], b, m).astype(jnp.bfloat16)

    return pl.pallas_call(
        body,
        in_specs=[VMEM] * 4,
        out_specs=VMEM,
        out_shape=jax.ShapeDtypeStruct((2, m, TB), jnp.bfloat16),
        compiler_params=params(),
        name="wide_sum",
    )(*parts)


def middle_sum(parts, m):
    def body(*refs):
        for g in range(2):
            for b in range(4):
                store_coded(
                    refs[8 + 4 * g + b], [decoded_sum(refs[4 * g : 4 * g + 4], b, m)]
                )

    out = jax.ShapeDtypeStruct((m + PAD, TB), jnp.int16)
    return pl.pallas_call(
        body,
        in_specs=[VMEM] * 8,
        out_specs=[VMEM] * 8,
        out_shape=[out] * 8,
        compiler_params=params(),
        name="middle_sum",
    )(*parts)


def last_sum(parts, m):
    def body(*refs):
        for g in range(2):
            refs[8][:, g * TB : (g + 1) * TB] = decoded_sum(
                refs[4 * g : 4 * g + 4], 0, m
            )

    return pl.pallas_call(
        body,
        in_specs=[VMEM] * 8,
        out_specs=VMEM,
        out_shape=jax.ShapeDtypeStruct((m, 2 * TB), F32),
        compiler_params=params(),
        name="last_sum",
    )(*parts)


def spread(value, axis):
    return [value] + [permute(value, axis, hop) for hop in HOPS]


def exchange(pieces, axis):
    return [pieces[0]] + [permute(p, axis, hop) for p, hop in zip(pieces[1:], HOPS)]


def per_device(tile_values, tile_rows, tile_cols, start_basis):
    tiles = tile_values[0, 0]
    rows = tile_rows[0, 0]
    cols = tile_cols[0, 0]
    rank = start_basis.shape[1]
    m = rank // CHUNKS
    z, core = lax.axis_index("row") // 2, lax.axis_index("row") % 2
    x, y = lax.axis_index("col") // 4, lax.axis_index("col") % 4

    odd = rows % 2
    dx, dy = (rows // 8 - x) % 4, (rows // 2 % 4 - y) % 4
    fx, fy = slot_from(dx), slot_from(dy)
    tx, ty = slot_to(dx), slot_to(dy)
    basis_slot = jnp.where(odd == 0, 4 * fy + fx, 16 + 4 * fx + fy)
    image_slot = jnp.where(odd == 0, 4 * tx + ty, 16 + 4 * ty + tx)
    away = jnp.where(cols // 8 == core, 0, 8)
    dz = (cols // 2 % 4 - z) % 4
    partial_slot = away + 2 * slot_to(dz) + cols % 2
    wide_slot = away + 2 * slot_from(dz) + cols % 2

    basis = start_basis.reshape(2, TB, rank).transpose(0, 2, 1)
    images = []
    for chunk in range(CHUNKS):
        own = basis[:, chunk * m : (chunk + 1) * m]
        line_x = jnp.stack(spread(own[0], "x"))
        line_y = jnp.stack(spread(own[1], "y"))
        gathered = spread(line_x, "y") + spread(line_y, "x")
        keep, send = first_product(basis_slot, partial_slot, tiles, gathered, m)
        pieces = pair_sum(keep, permute(send, "core", 1), m)
        wide = spread(wide_sum(exchange(pieces, "z"), m), "z")
        wide = wide + [permute(w, "core", 1) for w in wide]
        parts = second_product(image_slot, wide_slot, tiles, wide, m)
        parts = middle_sum(exchange(parts[:4], "x") + exchange(parts[4:], "y"), m)
        parts = exchange(parts[:4], "y") + exchange(parts[4:], "x")
        images.append(last_sum(parts, m))
    image = jnp.concatenate(images, axis=0)

    gram = lax.dot_general(
        image, image, (((1,), (1,)), ((), ())), precision=lax.Precision.HIGHEST
    )
    gram = gram + permute(gram, "core", 1)
    for axis in ("z", "x", "y"):
        own, up, down, over = spread(gram, axis)
        gram = own + over + (up + down)
    gram = gram / ORDER
    lower = jnp.linalg.cholesky(gram)
    new_basis = jax.scipy.linalg.solve_triangular(lower, image, lower=True).T
    return new_basis, lower.T


def solution(mesh):
    in_specs = (
        P("row", "col", None, None, None),
        P("row", "col", None),
        P("row", "col", None),
        P(("row", "col"), None),
    )
    out_specs = (P(("row", "col"), None), P())
    return jax.shard_map(
        per_device, mesh=mesh, in_specs=in_specs, out_specs=out_specs, check_vma=False
    )
```

time: 664 us -> 432 us (0.65)
  waiting for transfers between devices: 322 us -> 221 us
  blocking collectives: 93 us -> 0 us
  local copies, waits for them, and re-layouts: 91.1 us -> 10 us
  matrix products: 75.5 us -> 4.93 us
  starting transfers between devices: 0.29 us -> 64.1 us
  Pallas kernels: 0 us -> 63.3 us
  between operations: 15.4 us -> 2.45 us
    ppermute x0 -> x45, waiting for transfers between devices: none -> 221 us  [permute(): return lax.ppermute(value, name, [(i, place(i)) for i in range(size)])]
    psum x1 -> x0, waiting for transfers between devices: 141 us -> none  [per_device(): gram_matrix = lax.psum(local_gram, ('row', 'col')) / ORDER]
    reduce_scatter x1 -> x0, waiting for transfers between devices: 108 us -> none  [per_device(): lax.psum_scatter(row_partial, 'col', scatter_dimension=0, tiled=True)]
    psum x1 -> x0, blocking collectives: 93 us -> none  [per_device(): wide_blocks = lax.psum(partial_value, 'row').astype(jnp.bfloat16)]
    all_gather x1 -> x0, waiting for transfers between devices: 72.6 us -> none  [per_device(): lax.all_gather(start_basis, 'col', axis=0, tiled=True)]
    dot_general x5 -> x1, matrix products: 73.2 us -> 2.6 us  [per_device(): lax.dot_general(image, image, (((1,), (1,)), ((), ())), precision=lax.Pre...]
    ppermute x0 -> x45, starting transfers between devices: none -> 64.1 us  [permute(): return lax.ppermute(value, name, [(i, place(i)) for i in range(size)])]
    pallas_call x0 -> x6, Pallas kernels: none -> 63.3 us  [the longest x1 23.3 us: second_product(): pl.pallas_call(body, grid_spec=pltpu.PrefetchScalarGridSpec(num_scalar_pr...]
  transfers between devices with their start and end apart: 3 -> 45, of which waited for: 3 -> 33; matrix products, arithmetic and copies ran while one was open for 1% -> 0% of each run, Pallas kernels for 0% -> 0%
where the time goes in v1:
time: 432 us; the launch traced here: 423 us
  waiting for transfers between devices  221 us (51%)
  starting transfers between devices  64.1 us (15%)
  Pallas kernels  63.3 us (15%)
  other arithmetic  56.7 us (13%)
  local copies, waits for them, and re-layouts  10 us (2%)
  matrix products  4.93 us (1%)
    ppermute x45, waiting for transfers between devices, permute(): return lax.ppermute(value, name, [(i, place(i)) for i in range(size)])  221 us
    ppermute x45, starting transfers between devices, permute(): return lax.ppermute(value, name, [(i, place(i)) for i in range(size)])  64.1 us
    another operation x7, other arithmetic, per_device(): lower = jnp.linalg.cholesky(gram)  34.7 us
    pallas_call x1, Pallas kernels, second_product(): pl.pallas_call(body, grid_spec=pltpu.PrefetchScalarGridSpec(num_scalar_pr...  23.3 us
    pallas_call x1, Pallas kernels, first_product(): pl.pallas_call(body, grid_spec=pltpu.PrefetchScalarGridSpec(num_scalar_pr...  20.5 us
    another operation x2, other arithmetic, per_device(): new_basis = jax.scipy.linalg.solve_triangular(lower, image, lower=True).T  19.7 us
  transfers between devices with their start and end apart: 45, of which 33 were waited for; matrix products, arithmetic and copies ran while one was open for 0% of the time, Pallas kernels for 0%

profile of v1, /device:TPU:0, one launch (start us, length us, event | category | flops | bytes accessed | tf_op | source)
XLA Modules:
  0.0 422.9 jit_solution(13530498830218982379)
XLA Ops:
  7.2 5.6 %collective-permute-done.2 = bf16[256,512]{1,0:T(8,128)(2,1)S(1)} collective-permute-done((bf16[256,512]{1,0:T(8,128)(2,1)S(1)}, bf16[256,512]{1,0:T(8,128)(2,1)S(1)}, u32[]{:S(2)}, u32[]{:S(2)}) %collective-permute-start.2) | collective-permute-done | bytes 262176 | tf_op jit(solution)/shard_map/ppermute | solution.py:34
  12.8 4.7 %collective-permute-done.1 = bf16[256,512]{1,0:T(8,128)(2,1)S(1)} collective-permute-done((bf16[256,512]{1,0:T(8,128)(2,1)S(1)}, bf16[256,512]{1,0:T(8,128)(2,1)S(1)}, u32[]{:S(2)}, u32[]{:S(2)}) %collective-permute-start.1) | collective-permute-done | bytes 262176 | tf_op jit(solution)/shard_map/ppermute | solution.py:34
  26.7 25.1 %collective-permute-done.8 = bf16[256,512]{1,0:T(8,128)(2,1)S(1)} collective-permute-done((bf16[256,512]{1,0:T(8,128)(2,1)S(1)}, bf16[256,512]{1,0:T(8,128)(2,1)S(1)}, u32[]{:S(2)}, u32[]{:S(2)}) %collective-permute-start.8) | collective-permute-done | bytes 262176 | tf_op jit(solution)/shard_map/ppermute | solution.py:34
  61.0 17.7 %collective-permute-done.5.rest_3_ = bf16[4,256,512]{2,1,0:T(8,128)(2,1)} collective-permute-done((bf16[4,256,512]{2,1,0:T(8,128)(2,1)S(1)}, bf16[4,256,512]{2,1,0:T(8,128)(2,1)}, u32[]{:S(2)}, u32[]{:S(2)}) %collective-permute-start.5) | collective-permute-done | bytes 1048608 | tf_op jit(solution)/shard_map/ppermute | solution.py:34
  83.0 21.4 %collective-permute-done.11.rest_7_ = bf16[4,256,512]{2,1,0:T(8,128)(2,1)} collective-permute-done((bf16[4,256,512]{2,1,0:T(8,128)(2,1)S(1)}, bf16[4,256,512]{2,1,0:T(8,128)(2,1)}, u32[]{:S(2)}, u32[]{:S(2)}) %collective-permute-start.11) | collective-permute-done | bytes 1048608 | tf_op jit(solution)/shard_map/ppermute | solution.py:34
  104.4 20.5 %first_product.1 = (f32[8,256,512]{2,1,0:T(8,128)}, f32[8,256,512]{2,1,0:T(8,128)}) custom-call(s32[40]{0:T(128)} %get-tuple-element.69.row_ref, s32[40]{0:T(128)} %get-tuple-element.86.col_ref, bf16[40,512,512]{2,1,0:T(8,128)(2,1)} %bitcast.109, bf16[4,256,512]{2,1,0:T(8,128)(2,1)} %copy-done.1, bf16[4,256,512]{2,1,0:T(8,128)(2,1)} %copy-done.6, ...), custom_call_target="tpu_custom_call" | custom-call | flops 5368709120 | bytes 37748736 | tf_op jit(solution)/shard_map/first_product/pallas_call | solution.py:115
  125.0 7.5 %collective-permute-done.12.other_ref = f32[8,256,512]{2,1,0:T(8,128)} collective-permute-done((f32[8,256,512]{2,1,0:T(8,128)}, f32[8,256,512]{2,1,0:T(8,128)}, u32[]{:S(2)}, u32[]{:S(2)}) %collective-permute-start.12) | collective-permute-done | bytes 4194336 | tf_op jit(solution)/shard_map/ppermute | solution.py:34
  132.5 5.8 %pair_sum.1 = (s16[528,512]{1,0:T(8,128)(2,1)}, s16[528,512]{1,0:T(8,128)(2,1)}, s16[528,512]{1,0:T(8,128)(2,1)}, s16[528,512]{1,0:T(8,128)(2,1)}) custom-call(f32[8,256,512]{2,1,0:T(8,128)} %get-tuple-element.24.keep_ref, f32[8,256,512]{2,1,0:T(8,128)} %collective-permute-done.12.other_ref), custom_call_target="tpu_custom_call" | custom-call | tf_op jit(solution)/shard_map/pair_sum/pallas_call | solution.py:207
  144.2 10.9 %collective-permute-done.13.refs_1_ = s16[528,512]{1,0:T(8,128)(2,1)S(1)} collective-permute-done((s16[528,512]{1,0:T(8,128)(2,1)}, s16[528,512]{1,0:T(8,128)(2,1)S(1)}, u32[]{:S(2)}, u32[]{:S(2)}) %collective-permute-start.13) | collective-permute-done | bytes 540704 | tf_op jit(solution)/shard_map/ppermute | solution.py:34
  155.1 11.0 %collective-permute-done.14.refs_2_ = s16[528,512]{1,0:T(8,128)(2,1)S(1)} collective-permute-done((s16[528,512]{1,0:T(8,128)(2,1)}, s16[528,512]{1,0:T(8,128)(2,1)S(1)}, u32[]{:S(2)}, u32[]{:S(2)}) %collective-permute-start.14) | collective-permute-done | bytes 540704 | tf_op jit(solution)/shard_map/ppermute | solution.py:34
  175.0 22.4 %collective-permute-done.16.rest_1_ = bf16[2,256,512]{2,1,0:T(8,128)(2,1)S(1)} collective-permute-done((bf16[2,256,512]{2,1,0:T(8,128)(2,1)}, bf16[2,256,512]{2,1,0:T(8,128)(2,1)S(1)}, u32[]{:S(2)}, u32[]{:S(2)}) %collective-permute-start.16) | collective-permute-done | bytes 524320 | tf_op jit(solution)/shard_map/ppermute | solution.py:34
  201.7 23.3 %second_product.1 = (s16[1040,512]{1,0:T(8,128)(2,1)}, s16[1040,512]{1,0:T(8,128)(2,1)}, s16[1040,512]{1,0:T(8,128)(2,1)}, s16[1040,512]{1,0:T(8,128)(2,1)}, s16...) custom-call(s32[40]{0:T(128)} %compare_select_fusion.24.row_ref, ...), custom_call_target="tpu_custom_call" | custom-call | flops 5368709120 | bytes 37748736 | tf_op jit(solution)/shard_map/second_product/pallas_call | solution.py:173
  231.7 21.1 %collective-permute-done.23.refs_1_ = s16[1040,512]{1,0:T(8,128)(2,1)S(1)} collective-permute-done((s16[1040,512]{1,0:T(8,128)(2,1)}, s16[1040,512]{1,0:T(8,128)(2,1)S(1)}, u32[]{:S(2)}, u32[]{:S(2)}) %collective-permute-start.23) | collective-permute-done | bytes 1064992 | tf_op jit(solution)/shard_map/ppermute | solution.py:34
  254.8 19.5 %collective-permute-done.24.refs_2_ = s16[1040,512]{1,0:T(8,128)(2,1)S(1)} collective-permute-done((s16[1040,512]{1,0:T(8,128)(2,1)}, s16[1040,512]{1,0:T(8,128)(2,1)S(1)}, u32[]{:S(2)}, u32[]{:S(2)}) %collective-permute-start.24) | collective-permute-done | bytes 1064992 | tf_op jit(solution)/shard_map/ppermute | solution.py:34
  278.7 7.7 %middle_sum.1 = (s16[272,512]{1,0:T(8,128)(2,1)}, s16[272,512]{1,0:T(8,128)(2,1)}, s16[272,512]{1,0:T(8,128)(2,1)}, s16[272,512]{1,0:T(8,128)(2,1)}, s16[272,512...) custom-call(s16[1040,512]{1,0:T(8,128)(2,1)} %get-tuple-element.30.refs_0_, ...), custom_call_target="tpu_custom_call" | custom-call | tf_op jit(solution)/shard_map/middle_sum/pallas_call | solution.py:251
  317.6 5.8 %collective-permute-done.37 = f32[256,256]{0,1:T(8,128)S(1)} collective-permute-done((f32[256,256]{0,1:T(8,128)S(1)}, f32[256,256]{0,1:T(8,128)S(1)}, u32[]{:S(2)}, u32[]{:S(2)}) %collective-permute-start.37) | collective-permute-done | bytes 262176 | tf_op jit(solution)/shard_map/ppermute | solution.py:34
  323.4 4.8 %collective-permute-done.38 = f32[256,256]{0,1:T(8,128)S(1)} collective-permute-done((f32[256,256]{0,1:T(8,128)S(1)}, f32[256,256]{0,1:T(8,128)S(1)}, u32[]{:S(2)}, u32[]{:S(2)}) %collective-permute-start.38) | collective-permute-done | bytes 262176 | tf_op jit(solution)/shard_map/ppermute | solution.py:34
  334.3 5.7 %collective-permute-done.40 = f32[256,256]{0,1:T(8,128)S(1)} collective-permute-done((f32[256,256]{0,1:T(8,128)S(1)}, f32[256,256]{0,1:T(8,128)S(1)}, u32[]{:S(2)}, u32[]{:S(2)}) %collective-permute-start.40) | collective-permute-done | bytes 262176 | tf_op jit(solution)/shard_map/ppermute | solution.py:34
  350.1 4.4 %collective-permute-done.43 = f32[256,256]{0,1:T(8,128)S(1)} collective-permute-done((f32[256,256]{0,1:T(8,128)S(1)}, f32[256,256]{0,1:T(8,128)S(1)}, u32[]{:S(2)}, u32[]{:S(2)}) %collective-permute-start.43) | collective-permute-done | bytes 262176 | tf_op jit(solution)/shard_map/ppermute | solution.py:34
  358.1 11.7 %cholesky.50 = f32[128,128]{1,0:T(8,128)S(1)} custom-call(f32[128,128]{1,0:T(8,128)S(1)} %cholesky.118), custom_call_target="Cholesky" | custom-call | tf_op jit(solution)/shard_map/jit(cholesky)/cholesky | solution.py:331
  369.9 9.8 %custom-call.15 = f32[1,128,128]{1,2,0:T(8,128)S(1)} custom-call(f32[1,128,128]{2,1,0:T(8,128)S(1)} %get-tuple-element.83), custom_call_target="InvertDiagBlocksLowerTriangular" | custom-call | tf_op jit(solution)/shard_map/jit(cholesky)/cholesky | solution.py:331
  380.2 11.7 %cholesky.105 = f32[128,128]{1,0:T(8,128)S(1)} custom-call(f32[128,128]{1,0:T(8,128)S(1)} %convolution_subtract_fusion), custom_call_target="Cholesky" | custom-call | tf_op jit(solution)/shard_map/jit(cholesky)/cholesky | solution.py:331
  394.7 4.2 while.1
  398.9 19.7 %custom-call.16 = f32[2,128,128]{1,2,0:T(8,128)S(1)} custom-call(f32[2,128,128]{2,1,0:T(8,128)S(1)} %get-tuple-element.53), custom_call_target="InvertDiagBlocksLowerTriangular" | custom-call | tf_op jit(solution)/shard_map/jit(_solve_triangular)/triangular_solve | solution.py:332
  (165 shorter events, 122.4 us)
Async XLA Ops:
  17.6 40.9 %collective-permute-start.3 = (bf16[4,256,512]{2,1,0:T(8,128)(2,1)S(1)}, bf16[4,256,512]{2,1,0:T(8,128)(2,1)S(1)}, u32[]{:S(2)}, u32[]{:S(2)}) collective-permute-start(bf16[4,256,512]{2,1,0:T(8,128)(2,1)S(1)} %pad_maximum_fusion.rest_0_), channel_id=1, source_target_pairs={{0,1},{1,2},{2,3},{3,0},{4,5},{5,6},{6,7},{7,4},{8,9},{9,10},{10,1... | collective-permute-start | bytes 3145736 | tf_op jit(solution)/shard_map/ppermute | solution.py:34
  19.2 32.6 %collective-permute-start.8 = (bf16[256,512]{1,0:T(8,128)(2,1)S(1)}, bf16[256,512]{1,0:T(8,128)(2,1)S(1)}, u32[]{:S(2)}, u32[]{:S(2)}) collective-permute-start(bf16[256,512]{1,0:T(8,128)(2,1)S(1)} %get-tuple-element.76), channel_id=1, source_target_pairs={{0,2},{1,3},{2,0},{3,1},{4,6},{5,7},{6,4},{7,5},{8,10},{9,11},{10,... | collective-permute-start | bytes 786440 | tf_op jit(solution)/shard_map/ppermute | solution.py:34
  22.1 30.3 %collective-permute-start.7 = (bf16[256,512]{1,0:T(8,128)(2,1)S(1)}, bf16[256,512]{1,0:T(8,128)(2,1)S(1)}, u32[]{:S(2)}, u32[]{:S(2)}) collective-permute-start(bf16[256,512]{1,0:T(8,128)(2,1)S(1)} %get-tuple-element.76), channel_id=1, source_target_pairs={{0,3},{1,0},{2,1},{3,2},{4,7},{5,4},{6,5},{7,6},{8,11},{9,8},{10,9... | collective-permute-start | bytes 786440 | tf_op jit(solution)/shard_map/ppermute | solution.py:34
  23.5 31.5 %collective-permute-start.6 = (bf16[256,512]{1,0:T(8,128)(2,1)S(1)}, bf16[256,512]{1,0:T(8,128)(2,1)S(1)}, u32[]{:S(2)}, u32[]{:S(2)}) collective-permute-start(bf16[256,512]{1,0:T(8,128)(2,1)S(1)} %get-tuple-element.76), channel_id=1, source_target_pairs={{0,1},{1,2},{2,3},{3,0},{4,5},{5,6},{6,7},{7,4},{8,9},{9,10},{10,1... | collective-permute-start | bytes 786440 | tf_op jit(solution)/shard_map/ppermute | solution.py:34
  24.2 36.9 %collective-permute-start.4 = (bf16[4,256,512]{2,1,0:T(8,128)(2,1)S(1)}, bf16[4,256,512]{2,1,0:T(8,128)(2,1)}, u32[]{:S(2)}, u32[]{:S(2)}) collective-permute-start(bf16[4,256,512]{2,1,0:T(8,128)(2,1)S(1)} %pad_maximum_fusion.rest_0_), channel_id=1, source_target_pairs={{0,3},{1,0},{2,1},{3,2},{4,7},{5,4},{6,5},{7,6},{8,11},{9,8},{10,9... | collective-permute-start | bytes 3145736 | tf_op jit(solution)/shard_map/ppermute | solution.py:34
  51.8 26.9 %collective-permute-start.5 = (bf16[4,256,512]{2,1,0:T(8,128)(2,1)S(1)}, bf16[4,256,512]{2,1,0:T(8,128)(2,1)}, u32[]{:S(2)}, u32[]{:S(2)}) collective-permute-start(bf16[4,256,512]{2,1,0:T(8,128)(2,1)S(1)} %pad_maximum_fusion.rest_0_), channel_id=1, source_target_pairs={{0,2},{1,3},{2,0},{3,1},{4,6},{5,7},{6,4},{7,5},{8,10},{9,11},{10,... | collective-permute-start | bytes 3145736 | tf_op jit(solution)/shard_map/ppermute | solution.py:34
  55.2 26.2 %collective-permute-start.9 = (bf16[4,256,512]{2,1,0:T(8,128)(2,1)S(1)}, bf16[4,256,512]{2,1,0:T(8,128)(2,1)}, u32[]{:S(2)}, u32[]{:S(2)}) collective-permute-start(bf16[4,256,512]{2,1,0:T(8,128)(2,1)S(1)} %pad_maximum_fusion.1.rest_4_), channel_id=1, source_target_pairs={{0,4},{1,5},{2,6},{3,7},{4,8},{5,9},{6,10},{7,11},{8,12},{9,13},{1... | collective-permute-start | bytes 3145736 | tf_op jit(solution)/shard_map/ppermute | solution.py:34
  56.8 26.2 %collective-permute-start.10 = (bf16[4,256,512]{2,1,0:T(8,128)(2,1)S(1)}, bf16[4,256,512]{2,1,0:T(8,128)(2,1)}, u32[]{:S(2)}, u32[]{:S(2)}) collective-permute-start(bf16[4,256,512]{2,1,0:T(8,128)(2,1)S(1)} %pad_maximum_fusion.1.rest_4_), channel_id=1, source_target_pairs={{0,12},{1,13},{2,14},{3,15},{4,0},{5,1},{6,2},{7,3},{8,4},{9,5},{1... | collective-permute-start | bytes 3145736 | tf_op jit(solution)/shard_map/ppermute | solution.py:34
  58.5 45.9 %collective-permute-start.11 = (bf16[4,256,512]{2,1,0:T(8,128)(2,1)S(1)}, bf16[4,256,512]{2,1,0:T(8,128)(2,1)}, u32[]{:S(2)}, u32[]{:S(2)}) collective-permute-start(bf16[4,256,512]{2,1,0:T(8,128)(2,1)S(1)} %pad_maximum_fusion.1.rest_4_), channel_id=1, source_target_pairs={{0,8},{1,9},{2,10},{3,11},{4,12},{5,13},{6,14},{7,15},{8,0},{9,1},... | collective-permute-start | bytes 3145736 | tf_op jit(solution)/shard_map/ppermute | solution.py:34
  138.3 16.8 %collective-permute-start.13 = (s16[528,512]{1,0:T(8,128)(2,1)}, s16[528,512]{1,0:T(8,128)(2,1)S(1)}, u32[]{:S(2)}, u32[]{:S(2)}) collective-permute-start(s16[528,512]{1,0:T(8,128)(2,1)} %get-tuple-element.27), channel_id=1, source_target_pairs={{0,32},{16,48},{32,64},{48,80},{64,96},{80,112},{96,0},{112,16},{1... | collective-permute-start | bytes 1622024 | tf_op jit(solution)/shard_map/ppermute | solution.py:34
  140.2 25.9 %collective-permute-start.14 = (s16[528,512]{1,0:T(8,128)(2,1)}, s16[528,512]{1,0:T(8,128)(2,1)S(1)}, u32[]{:S(2)}, u32[]{:S(2)}) collective-permute-start(s16[528,512]{1,0:T(8,128)(2,1)} %get-tuple-element.28), channel_id=1, source_target_pairs={{0,96},{16,112},{32,0},{48,16},{64,32},{80,48},{96,64},{112,80},{1... | collective-permute-start | bytes 1622024 | tf_op jit(solution)/shard_map/ppermute | solution.py:34
  142.4 25.5 %collective-permute-start.15 = (s16[528,512]{1,0:T(8,128)(2,1)}, s16[528,512]{1,0:T(8,128)(2,1)S(1)}, u32[]{:S(2)}, u32[]{:S(2)}) collective-permute-start(s16[528,512]{1,0:T(8,128)(2,1)} %get-tuple-element.29), channel_id=1, source_target_pairs={{0,64},{16,80},{32,96},{48,112},{64,0},{80,16},{96,32},{112,48},{1... | collective-permute-start | bytes 1622024 | tf_op jit(solution)/shard_map/ppermute | solution.py:34
  171.6 25.8 %collective-permute-start.16 = (bf16[2,256,512]{2,1,0:T(8,128)(2,1)}, bf16[2,256,512]{2,1,0:T(8,128)(2,1)S(1)}, u32[]{:S(2)}, u32[]{:S(2)}) collective-permute-start(bf16[2,256,512]{2,1,0:T(8,128)(2,1)} %wide_sum.1.rest_0_), channel_id=1, source_target_pairs={{0,32},{16,48},{32,64},{48,80},{64,96},{80,112},{96,0},{112,16},{1... | collective-permute-start | bytes 1572872 | tf_op jit(solution)/shard_map/ppermute | solution.py:34
  172.8 24.7 %collective-permute-start.17 = (bf16[2,256,512]{2,1,0:T(8,128)(2,1)}, bf16[2,256,512]{2,1,0:T(8,128)(2,1)S(1)}, u32[]{:S(2)}, u32[]{:S(2)}) collective-permute-start(bf16[2,256,512]{2,1,0:T(8,128)(2,1)} %wide_sum.1.rest_0_), channel_id=1, source_target_pairs={{0,96},{16,112},{32,0},{48,16},{64,32},{80,48},{96,64},{112,80},{1... | collective-permute-start | bytes 1572872 | tf_op jit(solution)/shard_map/ppermute | solution.py:34
  174.9 23.1 %collective-permute-start.18 = (bf16[2,256,512]{2,1,0:T(8,128)(2,1)}, bf16[2,256,512]{2,1,0:T(8,128)(2,1)S(1)}, u32[]{:S(2)}, u32[]{:S(2)}) collective-permute-start(bf16[2,256,512]{2,1,0:T(8,128)(2,1)} %wide_sum.1.rest_0_), channel_id=1, source_target_pairs={{0,64},{16,80},{32,96},{48,112},{64,0},{80,16},{96,32},{112,48},{1... | collective-permute-start | bytes 1572872 | tf_op jit(solution)/shard_map/ppermute | solution.py:34
  175.0 24.3 %collective-permute-start.19 = (bf16[2,256,512]{2,1,0:T(8,128)(2,1)}, bf16[2,256,512]{2,1,0:T(8,128)(2,1)S(1)}, u32[]{:S(2)}, u32[]{:S(2)}) collective-permute-start(bf16[2,256,512]{2,1,0:T(8,128)(2,1)} %wide_sum.1.rest_0_), channel_id=1, source_target_pairs={{0,16},{16,0},{32,48},{48,32},{64,80},{80,64},{96,112},{112,96},{1... | collective-permute-start | bytes 1572872 | tf_op jit(solution)/shard_map/ppermute | solution.py:34
  225.0 27.8 %collective-permute-start.23 = (s16[1040,512]{1,0:T(8,128)(2,1)}, s16[1040,512]{1,0:T(8,128)(2,1)S(1)}, u32[]{:S(2)}, u32[]{:S(2)}) collective-permute-start(s16[1040,512]{1,0:T(8,128)(2,1)} %get-tuple-element.31), channel_id=1, source_target_pairs={{0,4},{1,5},{2,6},{3,7},{4,8},{5,9},{6,10},{7,11},{8,12},{9,13},{1... | collective-permute-start | bytes 3194888 | tf_op jit(solution)/shard_map/ppermute | solution.py:34
  226.3 48.1 %collective-permute-start.24 = (s16[1040,512]{1,0:T(8,128)(2,1)}, s16[1040,512]{1,0:T(8,128)(2,1)S(1)}, u32[]{:S(2)}, u32[]{:S(2)}) collective-permute-start(s16[1040,512]{1,0:T(8,128)(2,1)} %get-tuple-element.32), channel_id=1, source_target_pairs={{0,12},{1,13},{2,14},{3,15},{4,0},{5,1},{6,2},{7,3},{8,4},{9,5},{1... | collective-permute-start | bytes 3194888 | tf_op jit(solution)/shard_map/ppermute | solution.py:34
  228.3 46.7 %collective-permute-start.25 = (s16[1040,512]{1,0:T(8,128)(2,1)}, s16[1040,512]{1,0:T(8,128)(2,1)S(1)}, u32[]{:S(2)}, u32[]{:S(2)}) collective-permute-start(s16[1040,512]{1,0:T(8,128)(2,1)} %get-tuple-element.33), channel_id=1, source_target_pairs={{0,8},{1,9},{2,10},{3,11},{4,12},{5,13},{6,14},{7,15},{8,0},{9,1},... | collective-permute-start | bytes 3194888 | tf_op jit(solution)/shard_map/ppermute | solution.py:34
  228.4 46.6 %collective-permute-start.26 = (s16[1040,512]{1,0:T(8,128)(2,1)}, s16[1040,512]{1,0:T(8,128)(2,1)}, u32[]{:S(2)}, u32[]{:S(2)}) collective-permute-start(s16[1040,512]{1,0:T(8,128)(2,1)} %get-tuple-element.35), channel_id=1, source_target_pairs={{0,1},{1,2},{2,3},{3,0},{4,5},{5,6},{6,7},{7,4},{8,9},{9,10},{10,1... | collective-permute-start | bytes 3194888 | tf_op jit(solution)/shard_map/ppermute | solution.py:34
  228.8 46.2 %collective-permute-start.27 = (s16[1040,512]{1,0:T(8,128)(2,1)}, s16[1040,512]{1,0:T(8,128)(2,1)}, u32[]{:S(2)}, u32[]{:S(2)}) collective-permute-start(s16[1040,512]{1,0:T(8,128)(2,1)} %get-tuple-element.36), channel_id=1, source_target_pairs={{0,3},{1,0},{2,1},{3,2},{4,7},{5,4},{6,5},{7,6},{8,11},{9,8},{10,9... | collective-permute-start | bytes 3194888 | tf_op jit(solution)/shard_map/ppermute | solution.py:34
  252.8 25.9 %collective-permute-start.28 = (s16[1040,512]{1,0:T(8,128)(2,1)}, s16[1040,512]{1,0:T(8,128)(2,1)}, u32[]{:S(2)}, u32[]{:S(2)}) collective-permute-start(s16[1040,512]{1,0:T(8,128)(2,1)} %get-tuple-element.37), channel_id=1, source_target_pairs={{0,2},{1,3},{2,0},{3,1},{4,6},{5,7},{6,4},{7,5},{8,10},{9,11},{10,... | collective-permute-start | bytes 3194888 | tf_op jit(solution)/shard_map/ppermute | solution.py:34
  286.8 13.3 %collective-permute-start.30 = (s16[272,512]{1,0:T(8,128)(2,1)}, s16[272,512]{1,0:T(8,128)(2,1)S(1)}, u32[]{:S(2)}, u32[]{:S(2)}) collective-permute-start(s16[272,512]{1,0:T(8,128)(2,1)} %get-tuple-element.40), channel_id=1, source_target_pairs={{0,3},{1,0},{2,1},{3,2},{4,7},{5,4},{6,5},{7,6},{8,11},{9,8},{10,9... | collective-permute-start | bytes 835592 | tf_op jit(solution)/shard_map/ppermute | solution.py:34
  314.4 13.7 %collective-permute-start.38 = (f32[256,256]{0,1:T(8,128)S(1)}, f32[256,256]{0,1:T(8,128)S(1)}, u32[]{:S(2)}, u32[]{:S(2)}) collective-permute-start(f32[256,256]{0,1:T(8,128)S(1)} %add.162), channel_id=1, source_target_pairs={{0,96},{16,112},{32,0},{48,16},{64,32},{80,48},{96,64},{112,80},{1... | collective-permute-start | bytes 786440 | tf_op jit(solution)/shard_map/ppermute | solution.py:34
  (46 other events, 470.8 us)
